TPU v7x, 32 devices: a whole 2x2x4 slice. The times are simulated.
32 devices in a mesh: row: 8 (over z, core), col: 4 (over y, x).
Axes of the slice: x: 2, y: 2, z: 4, core: 2. Of those that a mesh axis runs over, the one named last changes fastest.
Arguments:
- a_tiles: bfloat16 [8, 4, 2, 16, 128, 128], P('row', 'col'), may hold values from 0 to 0.25
- a_index: int32 [8, 4, 2, 16], P('row', 'col'), may hold values from 0 to 127, as said below
- a_count: int32 [8, 4, 2], P('row', 'col'), may hold values from 1 to 16
- b_tiles: bfloat16 [8, 4, 16, 128, 128], P('row', 'col'), may hold values from 0 to 0.25
- b_index: int32 [8, 4, 16], P('row', 'col'), may hold values from 0 to 127, as said below
- b_count: int32 [8, 4], P('row', 'col'), may hold values from 1 to 16
- c_partial: float32 [4096, 2048], P('row', 'col'), may hold values from 0.25 to 60, as said below
- prune_mask: int32 [32, 16], P('row', 'col'), may hold values from 0 to 1, as said below
Outputs:
- renormed: float32 [4096, 2048], P('row', 'col')
Inputs may be any that keep to these rules, and one draw needn't show every extreme that they name: `a_index`: within one device and section the slots are distinct. `b_index`: within one device the slots are distinct. `prune_mask`: every block column keeps at least one tile. `c_partial`: positive entries.
All inputs are finite; a program needn't handle non-finite values.
Results may differ from a plain program's by a relative error of at most 0.0003.
Values may be sent and summed in bfloat16 or wider, within the bound.
A program may use at most 64 MiB of HBM per device.

v0:
```python
import jax
import jax.numpy as jnp
from jax import lax
from jax.sharding import PartitionSpec as P

MB = 4
NB = 4
W = 32
KA = 16
KB = 16
SECTIONS = 2


def spread(array, axis, root):
    mine = lax.axis_index(axis) == root
    return lax.psum(jnp.where(mine, array, jnp.zeros_like(array)), axis)


def place_tiles(tiles, slots, count_slots):
    onehot = (slots[:, None] == jnp.arange(count_slots)[None, :]).astype(jnp.bfloat16)
    dense = jnp.einsum("ap,auv->puv", onehot, tiles, preferred_element_type=jnp.float32)
    return dense.astype(jnp.bfloat16)


def section_product(left_tiles, left_slots, right_tiles, right_slots):
    tile = left_tiles.shape[-1]
    left_dense = place_tiles(left_tiles, left_slots, MB * W)
    left_panel = (
        left_dense.reshape(MB, W, tile, tile).transpose(0, 2, 1, 3).reshape(MB * tile, W * tile)
    )
    right_dense = place_tiles(right_tiles, right_slots, W * NB)
    right_panel = (
        right_dense.reshape(W, NB, tile, tile).transpose(0, 2, 1, 3).reshape(W * tile, NB * tile)
    )
    return jnp.dot(left_panel, right_panel, preferred_element_type=jnp.float32)


def local(a_tiles, a_index, a_count, b_tiles, b_index, b_count, c_partial, prune_mask):
    n_row = lax.axis_size("row")
    n_col = lax.axis_size("col")
    left_all = a_tiles[0, 0]
    left_slots = jnp.where(jnp.arange(KA)[None, :] < a_count[0, 0][:, None], a_index[0, 0], -1)
    right_slots = jnp.where(jnp.arange(KB) < b_count[0, 0], b_index[0, 0], -1)
    expanded = c_partial
    for section in range(SECTIONS):
        section_tiles, section_slots = (
            spread(left_all[section], "col", n_col - 1),
            spread(left_slots[section], "col", n_col - 1),
        )
        got_tiles, got_slots = (
            spread(b_tiles[0, 0], "row", n_row - 2 + section),
            spread(right_slots, "row", n_row - 2 + section),
        )
        expanded = expanded + section_product(section_tiles, section_slots, got_tiles, got_slots)
    tile = a_tiles.shape[-1]
    keep = prune_mask.astype(jnp.float32)[:, None, :, None]
    kept = (expanded * expanded).reshape(MB, tile, NB, tile) * keep
    partial_value = jnp.sum(kept, axis=(0, 1)).reshape(NB * tile)
    colsum = lax.psum(partial_value, "row")
    total_rows = n_row * MB * tile
    return kept.reshape(MB * tile, NB * tile) * (total_rows / colsum)[None, :]


def solution(mesh):
    return jax.shard_map(
        local,
        mesh=mesh,
        in_specs=(
            P("row", "col", None, None, None, None),
            P("row", "col", None, None),
            P("row", "col", None),
            P("row", "col", None, None, None),
            P("row", "col", None),
            P("row", "col"),
            P("row", "col"),
            P("row", "col"),
        ),
        out_specs=P("row", "col"),
        check_vma=False,
    )
```

profile of v0, /device:TPU:0, one launch (start us, length us, event | category | flops | bytes accessed | tf_op | source)
XLA Modules:
  0.0 162.9 jit_solution(4770668057268410517)
XLA Ops:
  6.5 0.0 copy-start.6
  6.5 0.0 copy-start.5
  6.5 0.0 copy-start.4
  6.5 0.0 copy-start.7
  6.5 0.0 all-reduce.7.cloned.1.call-start
  6.6 2.4 %select_bitcast_fusion.1 = (bf16[16,128,128]{2,0,1:T(8,128)(2,1)}, bf16[16,128,128]{2,0,1:T(8,128)(2,1)}) fusion(pred[]{:T(512)S(6)} %eq.34, bf16[1,1,16,128,128]{4,3,2,1,0:T(8,128)(2,1)} %param.11, pred[]{:T(512)S(6)} %eq.77), kind=kLoop, calls=%fused_computation.24 | loop fusion | flops 524288 | bytes 1572866 | tf_op jit(solution)/shard_map/jit(_where)/select_n | solution.py:16
  9.0 0.0 all-reduce.7.cloned.1.call-update
  9.0 0.0 all-reduce.9.cloned.1.call-start
  9.0 1.3 fusion.46
  10.3 1.6 fusion.30
  11.9 0.0 all-reduce.9.cloned.1.call-update
  11.9 0.0 copy-done.6
  11.9 0.0 copy-done.5
  11.9 0.1 compare_select_fusion.1
  12.0 8.8 %all-reduce.1 = (s32[16]{0:T(128)S(1)}, s32[16]{0:T(128)S(1)}) all-reduce(s32[16]{0:T(128)S(1)} %get-tuple-element.18, s32[16]{0:T(128)S(1)} %get-tuple-element.17), channel_id=1, replica_groups=mesh['row'=8,'col'=4] {'col'}, use_global_device_ids=true, to_apply=%region_4.5 | all-reduce | flops 32 | bytes 256 | tf_op jit(solution)/shard_map/psum | solution.py:16
  21.5 0.0 copy-done.4
  21.5 0.0 copy-done.7
  21.6 9.3 %all-reduce = (s32[16]{0:T(128)S(1)}, s32[16]{0:T(128)S(1)}) all-reduce(s32[16]{0:T(128)S(1)} %get-tuple-element.20, s32[16]{0:T(128)S(1)} %get-tuple-element.19), channel_id=1, replica_groups=mesh['row'=8,'col'=4] {'row'}, use_global_device_ids=true, to_apply=%region_6.7 | all-reduce | flops 32 | bytes 256 | tf_op jit(solution)/shard_map/psum | solution.py:16
  30.8 40.7 %all-reduce.7.cloned.1.call-done = (bf16[16,128,128]{2,0,1:T(8,128)(2,1)}, bf16[16,128,128]{2,0,1:T(8,128)(2,1)}) async-done(((bf16[16,128,128]{2,0,1:T(8,128)(2,1)}, bf16[16,128,128]{2,0,1:T(8,128)(2,1)}), (bf16[16,128,128]{2,0,1:T(8,128)(2,1)}, bf16[16,128,128]{2,0,1:T(8,128)(2,1)})) %all-reduce.7.cloned.1.call-update) | async-done | bytes 1048592 | tf_op jit(solution)/shard_map/psum | solution.py:16
  71.5 4.4 %convolution_convert_fusion = bf16[128,128,128]{2,0,1:T(8,128)(2,1)} fusion(bf16[16,128,128]{2,0,1:T(8,128)(2,1)} %get-tuple-element.9, s32[16]{0:T(128)S(1)} %get-tuple-element.5), kind=kOutput, calls=%fused_computation.10 | convolution fusion | flops 69208064 | bytes 4718656 | tf_op jit(solution)/shard_map/ap,auv->puv/dot_general | solution.py:21
  75.9 0.0 copy-start.2
  75.9 8.6 %copy.20 = bf16[32,4,128,128]{2,0,3,1:T(8,128)(2,1)} copy(bf16[32,4,128,128]{3,1,0,2:T(4,128)(2,1)} %bitcast.95) | data formatting | bytes 8388608 | tf_op jit(solution)/shard_map/reshape | solution.py:33
  84.4 0.0 copy-done.2
  84.4 3.3 %convolution_convert_fusion.2 = bf16[128,128,128]{2,0,1:T(8,128)(2,1)} fusion(bf16[16,128,128]{2,0,1:T(8,128)(2,1)S(1)} %copy-done.2, s32[16]{0:T(128)S(1)} %get-tuple-element.6), kind=kOutput, calls=%fused_computation.12 | convolution fusion | flops 69208064 | bytes 4718656 | tf_op jit(solution)/shard_map/ap,auv->puv/dot_general | solution.py:21
  87.8 8.6 %copy.16 = bf16[32,4,128,128]{2,0,3,1:T(8,128)(2,1)} copy(bf16[32,4,128,128]{3,1,0,2:T(4,128)(2,1)} %bitcast.96) | data formatting | bytes 8388608 | tf_op jit(solution)/shard_map/reshape | solution.py:33
  96.3 30.0 %all-reduce.9.cloned.1.call-done = (bf16[16,128,128]{2,0,1:T(8,128)(2,1)}, bf16[16,128,128]{2,0,1:T(8,128)(2,1)}) async-done(((bf16[16,128,128]{2,0,1:T(8,128)(2,1)}, bf16[16,128,128]{2,0,1:T(8,128)(2,1)}), (bf16[16,128,128]{2,0,1:T(8,128)(2,1)}, bf16[16,128,128]{2,0,1:T(8,128)(2,1)})) %all-reduce.9.cloned.1.call-update) | async-done | bytes 1048592 | tf_op jit(solution)/shard_map/psum | solution.py:16
  126.3 2.4 %convolution_convert_fusion.1 = bf16[128,128,128]{2,0,1:T(8,128)(2,1)S(1)} fusion(bf16[16,128,128]{2,0,1:T(8,128)(2,1)} %get-tuple-element.11, s32[16]{0:T(128)S(1)} %get-tuple-element.7), kind=kOutput, calls=%fused_computation.11 | convolution fusion | flops 69208064 | bytes 4718656 | tf_op jit(solution)/shard_map/ap,auv->puv/dot_general | solution.py:21
  128.7 0.0 copy-start.3
  128.7 0.8 copy.18
  129.5 0.2 copy-done.3
  129.7 1.4 convolution_convert_fusion.3
  131.1 0.0 copy-start
  131.1 0.8 copy.14
  131.9 1.4 copy-done
  133.3 0.0 copy-start.1
  133.3 0.0 copy-start.8
  133.3 2.5 %fusion = f32[512,512]{1,0:T(8,128)S(1)} fusion(bf16[64,8,32,128]{3,2,1,0:T(8,128)(2,1)S(1)} %bitcast.99, bf16[64,8,32,128]{3,2,1,0:T(8,128)(2,1)S(1)} %bitcast.101), kind=kOutput, calls=%fused_computation | convolution fusion | flops 2147483648 | bytes 9437184 | tf_op jit(solution)/shard_map/dot_general | solution.py:35
  135.8 0.2 mul.24
  136.0 0.0 copy-done.1
  136.0 0.0 copy-done.8
  136.1 2.5 %fusion.47 = (f32[512]{0:T(512)S(1)}, f32[512,512]{1,0:T(8,128)S(1)}) fusion(f32[64,8,4,128]{3,2,1,0:T(4,128)S(1)} %bitcast.103, f32[512,512]{1,0:T(8,128)S(1)} %fusion, f32[512,512]{1,0:T(8,128)S(1)} %copy-done.8, bf16[64,8,32,128]{3,2,1,0:T(8,128)(2,1)S(1)} %bitcast.100, bf16[64,8,32,128]{3,2,1,0:T(8,128)(2,1)S(1)} %bitcast.102), kind=kOutput, calls=%fused_computation.47 | convolution fusion | flops 2148793856 | bytes 12584960 | tf_op jit(solution)/shard_map/dot_general | solution.py:35
  138.6 16.4 %psum.71 = f32[512]{0:T(512)S(1)} all-reduce(f32[512]{0:T(512)S(1)} %get-tuple-element.21), channel_id=1, replica_groups=mesh['row'=8,'col'=4] {'row'}, use_global_device_ids=true, to_apply=%region_9.10 | all-reduce | flops 512 | bytes 4096 | tf_op jit(solution)/shard_map/psum | solution.py:59
  155.0 1.1 broadcast_multiply_fusion
  (4 shorter events, 0.0 us)
Async XLA Ops:
  6.5 5.4 %copy-start.6 = (s32[1,1,2]{2,1,0:T(1,128)S(1)}, s32[1,1,2]{2,1,0:T(1,128)}, u32[]{:S(2)}) copy-start(s32[1,1,2]{2,1,0:T(1,128)} %param.10) | copy-start | bytes 28
  6.5 5.4 %copy-start.5 = (s32[1,1,2,16]{3,2,1,0:T(2,128)S(1)}, s32[1,1,2,16]{3,2,1,0:T(2,128)}, u32[]{:S(2)}) copy-start(s32[1,1,2,16]{3,2,1,0:T(2,128)} %param.9) | copy-start | bytes 388
  6.5 15.0 %copy-start.4 = (s32[4,4]{1,0:T(4,128)S(1)}, s32[4,4]{1,0:T(4,128)}, u32[]{:S(2)}) copy-start(s32[4,4]{1,0:T(4,128)} %param.15) | copy-start | bytes 196
  6.5 15.0 %copy-start.7 = (s32[1,1,16]{2,1,0:T(1,128)S(1)}, s32[1,1,16]{2,1,0:T(1,128)}, u32[]{:S(2)}) copy-start(s32[1,1,16]{2,1,0:T(1,128)} %param.12) | copy-start | bytes 196
  6.5 64.9 %all-reduce.7.cloned.1.call-start = ((), (), s32[]{:S(2)}) async-start(), calls=%async_computation | async-start | bytes 2097152 | tf_op jit(solution)/shard_map/psum | solution.py:16
  9.0 117.3 %all-reduce.9.cloned.1.call-start = ((), (), s32[]{:S(2)}) async-start(), calls=%async_computation.1 | async-start | bytes 2097152 | tf_op jit(solution)/shard_map/psum | solution.py:16
  75.9 8.6 %copy-start.2 = (bf16[16,128,128]{2,0,1:T(8,128)(2,1)S(1)}, bf16[16,128,128]{2,0,1:T(8,128)(2,1)}, u32[]{:S(2)}) copy-start(bf16[16,128,128]{2,0,1:T(8,128)(2,1)} %get-tuple-element.10) | copy-start | bytes 1572868
  128.7 1.0 copy-start.3
  131.1 2.2 %copy-start = (bf16[32,4,128,128]{2,0,3,1:T(8,128)(2,1)S(1)}, bf16[32,4,128,128]{2,0,3,1:T(8,128)(2,1)}, u32[]{:S(2)}) copy-start(bf16[32,4,128,128]{2,0,3,1:T(8,128)(2,1)} %copy.20) | copy-start | bytes 12582916
  133.3 2.8 %copy-start.1 = (bf16[32,4,128,128]{2,0,3,1:T(8,128)(2,1)S(1)}, bf16[32,4,128,128]{2,0,3,1:T(8,128)(2,1)}, u32[]{:S(2)}) copy-start(bf16[32,4,128,128]{2,0,3,1:T(8,128)(2,1)} %copy.16) | copy-start | bytes 12582916
  133.3 2.8 %copy-start.8 = (f32[512,512]{1,0:T(8,128)S(1)}, f32[512,512]{1,0:T(8,128)}, u32[]{:S(2)}) copy-start(f32[512,512]{1,0:T(8,128)} %param.14) | copy-start | bytes 3145732
Sparse Core Ops, SparseCore 0:
  9.8 61.6 all-reduce.6
  74.5 51.6 all-reduce.8
where the time goes:
time: 163 us
  waiting for transfers between devices  70.7 us (43%)
  blocking collectives  34.5 us (21%)
  local copies, waits for them, and re-layouts  21.8 us (13%)
  matrix products  16.5 us (10%)
  between operations  14.2 us (9%)
  other arithmetic  5.16 us (3%)
    psum x2, waiting for transfers between devices, spread(): return lax.psum(jnp.where(mine, array, jnp.zeros_like(array)), axis)  70.6 us
    psum x2, blocking collectives, spread(): return lax.psum(jnp.where(mine, array, jnp.zeros_like(array)), axis)  18.1 us
    reshape x2, local copies, waits for them, and re-layouts, section_product(): right_dense.reshape(W, NB, tile, tile).transpose(0, 2, 1, 3)  17.1 us
    psum x1, blocking collectives, local(): colsum = lax.psum(partial_value, 'row')  16.4 us
    dot_general x4, matrix products, place_tiles(): jnp.einsum('ap,auv->puv', onehot, tiles, preferred_element_type=jnp.float32)  11.5 us
    dot_general x2, matrix products, section_product(): return jnp.dot(left_panel, right_panel, preferred_element_type=jnp.float32)  5.07 us
    select_n x4, other arithmetic, spread(): return lax.psum(jnp.where(mine, array, jnp.zeros_like(array)), axis)  3.97 us
  transfers between devices with their start and end apart: 2, of which 2 were waited for; matrix products, arithmetic and copies ran while one was open for 17% of the time, Pallas kernels for 0%

commit v1 on v0

v1 whole, which is shorter than its diff:
```python
import functools

import jax
import jax.numpy as jnp
from jax import lax
from jax.experimental import pallas as pl
from jax.experimental.pallas import tpu as pltpu
from jax.sharding import PartitionSpec as P

MB = 4
NB = 4
W = 32
KA = 16
KB = 16
SECTIONS = 2
TILE = 128
STEP = 2
PARTS = KA // 2 // STEP
MESH = pl.DeviceIdType.MESH


def grid_of(n_col):
    nx = max(d for d in range(1, n_col + 1) if n_col % d == 0 and d * d <= n_col)
    return n_col // nx, nx


def snake(index, outer, inner):
    o, i = index // inner, index % inner
    return o, (1 - o % 2) * i + (o % 2) * (inner - 1 - i)


def path_position(col, path, ny, nx):
    y, x = ny - 1 - col // nx, nx - 1 - col % nx
    if path == 0:
        return y * nx + (1 - y % 2) * x + (y % 2) * (nx - 1 - x)
    return x * ny + (1 - x % 2) * y + (x % 2) * (ny - 1 - y)


def path_column(position, path, ny, nx):
    if path == 0:
        y, x = snake(position, ny, nx)
    else:
        x, y = snake(position, nx, ny)
    return (ny - 1 - y) * nx + (nx - 1 - x)


def kernel(
    n_row, n_col, ai_ref, ac_ref, bi_ref, bc_ref, mask_ref, a_hbm, b_hbm, c_hbm,
    kept_hbm, scale_ref,
    lt0, lt1, rt0, rt1, ma, mb, table, table_smem, acc, sums,
    a_send, a_recv, b_send, b_recv, sib_send, sib_recv, ma_send, ma_recv, mb_send, mb_recv,
    cs_send, cs_recv, loc,
):
    row = lax.axis_index("row")
    col = lax.axis_index("col")
    pair, core = row // 2, row % 2
    last_pair = n_row // 2 - 1
    ny, nx = grid_of(n_col)
    lts, rts = (lt0, lt1), (rt0, rt1)
    total_rows = n_row * MB * TILE

    load_c = pltpu.make_async_copy(c_hbm, acc, loc.at[0])
    load_c.start()

    barrier = pltpu.get_barrier_semaphore()
    for d in range(1, n_row):
        pl.semaphore_signal(barrier, inc=1, device_id=((row + d) % n_row, col), device_id_type=MESH)
    for d in range(1, n_col):
        pl.semaphore_signal(barrier, inc=1, device_id=(row, (col + d) % n_col), device_id_type=MESH)

    lane = lax.broadcasted_iota(jnp.int32, (1, TILE), 1)

    @pl.when(col == n_col - 1)
    def _():
        for s in range(SECTIONS):
            count = ac_ref[0, 0, s]
            target = jnp.full((1, TILE), -2, jnp.int32)
            place = jnp.full((1, TILE), KA, jnp.int32)
            for a in range(KA):
                slot = ai_ref[0, 0, s, a]
                live = a < count
                inner = jnp.where(live, (slot % W) * NB, -64)
                block = jnp.where(live, slot // W, -1)
                target = jnp.where(lane // NB == a, inner + lane % NB, target)
                place = jnp.where(lane == block * KA + a, jnp.where(live, a, KA), place)
            ma[s : s + 1, :] = target
            ma[SECTIONS + s : SECTIONS + s + 1, :] = place

    for s in range(SECTIONS):

        @pl.when(row == n_row - SECTIONS + s)
        def _(s=s):
            count = bc_ref[0, 0]
            for b in range(KB):
                slot = jnp.where(b < count, bi_ref[0, 0, b], -1)
                mb[s, b : b + 1, :] = jnp.full((1, TILE), slot, jnp.int32)

    for s in range(SECTIONS):
        lts[s][KA] = jnp.zeros((TILE, TILE), jnp.bfloat16)
        rts[s][KB] = jnp.zeros((TILE, TILE), jnp.bfloat16)

    pl.semaphore_wait(barrier, n_row - 1 + n_col - 1)

    positions = [path_position(col, p, ny, nx) for p in range(2)]
    is_left_root = col == n_col - 1

    def next_col(p):
        return path_column((positions[p] + 1) % n_col, p, ny, nx)

    def a_copy(p, i, from_hbm):
        s, c = i // PARTS, i % PARTS
        tiles = pl.ds(p * (KA // 2) + c * STEP, STEP)
        return pltpu.make_async_remote_copy(
            src_ref=a_hbm.at[0, 0, s, tiles] if from_hbm else lts[s].at[tiles],
            dst_ref=lts[s].at[tiles],
            send_sem=a_send.at[p, i], recv_sem=a_recv.at[p, i],
            device_id=(row, next_col(p)), device_id_type=MESH,
        )

    def ma_copy():
        return pltpu.make_async_remote_copy(
            src_ref=ma, dst_ref=ma, send_sem=ma_send.at[0], recv_sem=ma_recv.at[0],
            device_id=(row, next_col(0)), device_id_type=MESH,
        )

    def a_local(s):
        return pltpu.make_async_copy(a_hbm.at[0, 0, s], lts[s].at[pl.ds(0, KA)], loc.at[1 + s])

    below = (pair - 1 + last_pair + 1) % (last_pair + 1)
    sibling = pair * 2 + 1 - core

    def b_root_copy(s, k, c):
        tiles = pl.ds(k * (KB // 2) + c * STEP, STEP)
        return pltpu.make_async_remote_copy(
            src_ref=b_hbm.at[0, 0, tiles], dst_ref=rts[s].at[tiles],
            send_sem=b_send.at[k * PARTS + c], recv_sem=b_recv.at[s * PARTS + c],
            device_id=(below * 2 + k, col), device_id_type=MESH,
        )

    def b_root_sibling(s):
        return pltpu.make_async_remote_copy(
            src_ref=b_hbm.at[0, 0], dst_ref=rts[s].at[pl.ds(0, KB)],
            send_sem=sib_send.at[0], recv_sem=sib_recv.at[s * PARTS],
            device_id=(sibling, col), device_id_type=MESH,
        )

    def mb_copy(s, target, sem):
        return pltpu.make_async_remote_copy(
            src_ref=mb.at[s], dst_ref=mb.at[s], send_sem=mb_send.at[sem], recv_sem=mb_recv.at[s],
            device_id=(target, col), device_id_type=MESH,
        )

    def b_tiles(i, k):
        return pl.ds(k * (KB // 2) + (i % PARTS) * STEP, STEP)

    def b_copy(i):
        ref = rts[i // PARTS].at[b_tiles(i, core)]
        return pltpu.make_async_remote_copy(
            src_ref=ref, dst_ref=ref, send_sem=b_send.at[i], recv_sem=b_recv.at[i],
            device_id=(below * 2 + core, col), device_id_type=MESH,
        )

    def sib_copy(i):
        ref = rts[i // PARTS].at[b_tiles(i, core)]
        return pltpu.make_async_remote_copy(
            src_ref=ref, dst_ref=ref, send_sem=sib_send.at[i], recv_sem=sib_recv.at[i],
            device_id=(sibling, col), device_id_type=MESH,
        )

    def sib_arrival(i):
        ref = rts[i // PARTS].at[b_tiles(i, 1 - core)]
        return pltpu.make_async_remote_copy(
            src_ref=ref, dst_ref=ref, send_sem=sib_send.at[i], recv_sem=sib_recv.at[i],
            device_id=(sibling, col), device_id_type=MESH,
        )

    def b_local(s):
        return pltpu.make_async_copy(b_hbm.at[0, 0], rts[s].at[pl.ds(0, KB)], loc.at[3])

    steps = SECTIONS * PARTS
    in_chain = pair < last_pair

    @pl.when(is_left_root)
    def _():
        ma_copy().start()
        for i in range(steps):
            for p in range(2):
                a_copy(p, i, True).start()
        for s in range(SECTIONS):
            a_local(s).start()

    for s in range(SECTIONS):

        @pl.when(row == n_row - SECTIONS + s)
        def _(s=s):
            for k in range(2):
                mb_copy(s, below * 2 + k, k).start()
            mb_copy(s, sibling, 2).start()
            for c in range(PARTS):
                for k in range(2):
                    b_root_copy(s, k, c).start()
            b_root_sibling(s).start()
            b_local(s).start()

    @pl.when(positions[0] > 0)
    def _():
        ma_copy().wait_recv()

        @pl.when(positions[0] < n_col - 1)
        def _():
            ma_copy().start()

    def forward(i):
        for p in range(2):

            @pl.when(positions[p] > 0)
            def _(p=p):
                a_copy(p, i, False).wait_recv()

                @pl.when(positions[p] < n_col - 1)
                def _():
                    a_copy(p, i, False).start()

        @pl.when(in_chain)
        def _():
            b_copy(i).wait_recv()

            @pl.when(pair > 0)
            def _():
                b_copy(i).start()

            sib_copy(i).start()

    def section_ready(s):
        @pl.when(is_left_root)
        def _():
            a_local(s).wait()

        @pl.when(in_chain)
        def _():
            for c in range(PARTS):
                sib_arrival(s * PARTS + c).wait_recv()

        @pl.when(row == n_row - SECTIONS + s)
        def _():
            b_local(s).wait()

        @pl.when(row == n_row - 1 - s)
        def _():
            b_root_sibling(s).wait_recv()

    for s in range(SECTIONS):

        @pl.when(in_chain)
        def _(s=s):
            mb_copy(s, below * 2 + core, s).wait_recv()

            @pl.when(pair > 0)
            def _():
                mb_copy(s, below * 2 + core, s).start()

        @pl.when(row == n_row - 1 - s)
        def _(s=s):
            mb_copy(s, sibling, s).wait_recv()

    row_id = lax.broadcasted_iota(jnp.int32, (KB, TILE), 0)
    for s in range(SECTIONS):
        hit = mb[s] == ma[s : s + 1, :]
        table[s : s + 1, :] = jnp.min(jnp.where(hit, row_id, KB), axis=0, keepdims=True)
    table[SECTIONS : 2 * SECTIONS, :] = ma[SECTIONS : 2 * SECTIONS, :]
    to_smem = pltpu.make_async_copy(table, table_smem, loc.at[4])
    to_smem.start()

    group = KA // PARTS

    def product(s, j):
        left = jnp.concatenate(
            [
                jnp.concatenate(
                    [lts[s][table_smem[SECTIONS + s, m * KA + j * group + a]] for a in range(group)],
                    axis=1,
                )
                for m in range(MB)
            ],
            axis=0,
        )
        right = jnp.concatenate(
            [
                jnp.concatenate(
                    [rts[s][table_smem[s, (j * group + a) * NB + n]] for n in range(NB)], axis=1
                )
                for a in range(group)
            ],
            axis=0,
        )
        acc[...] += jnp.dot(left, right, preferred_element_type=jnp.float32)

    for i in range(PARTS):
        forward(i)
    to_smem.wait()
    load_c.wait()
    for s in range(SECTIONS):
        section_ready(s)
        for j in range(PARTS):
            if s + 1 < SECTIONS:
                forward((s + 1) * PARTS + j)
            product(s, j)

    partial = jnp.zeros((1, NB * TILE), jnp.float32)
    for m in range(MB):
        keep = jnp.concatenate(
            [
                jnp.full((1, TILE), mask_ref[m, n].astype(jnp.float32), jnp.float32)
                for n in range(NB)
            ],
            axis=1,
        )
        block = acc[m * TILE : (m + 1) * TILE, :]
        kept = block * block * keep
        acc[m * TILE : (m + 1) * TILE, :] = kept
        partial = partial + jnp.sum(kept, axis=0, keepdims=True)
    store = pltpu.make_async_copy(acc, kept_hbm, loc.at[0])
    store.start()

    sums[row] = partial

    def cs_copy(target, slot):
        return pltpu.make_async_remote_copy(
            src_ref=sums.at[slot], dst_ref=sums.at[slot],
            send_sem=cs_send.at[target], recv_sem=cs_recv.at[slot],
            device_id=(target, col), device_id_type=MESH,
        )

    for d in range(1, n_row):
        cs_copy((row + d) % n_row, row).start()
    for d in range(1, n_row):
        source = (row + d) % n_row
        cs_copy(source, source).wait_recv()
    scale_ref[...] = total_rows / jnp.sum(sums[...], axis=0)

    for d in range(1, n_row):
        cs_copy((row + d) % n_row, row).wait_send()
    for p in range(2):

        @pl.when(positions[p] < n_col - 1)
        def _(p=p):
            for i in range(steps):
                a_copy(p, i, False).wait_send()

    @pl.when(positions[0] < n_col - 1)
    def _():
        ma_copy().wait_send()

    @pl.when(in_chain)
    def _():
        for i in range(steps):
            sib_copy(i).wait_send()

        @pl.when(pair > 0)
        def _():
            for i in range(steps):
                b_copy(i).wait_send()
            for s in range(SECTIONS):
                mb_copy(s, below * 2 + core, s).wait_send()

    for s in range(SECTIONS):

        @pl.when(row == n_row - SECTIONS + s)
        def _(s=s):
            for k in range(2):
                mb_copy(s, below * 2 + k, k).wait_send()
            mb_copy(s, sibling, 2).wait_send()
            for c in range(PARTS):
                for k in range(2):
                    b_root_copy(s, k, c).wait_send()
            b_root_sibling(s).wait_send()

    store.wait()


def local(n_row, n_col, a_tiles, a_index, a_count, b_tiles, b_index, b_count, c_partial, prune_mask):
    smem = pl.BlockSpec(memory_space=pltpu.SMEM)
    hbm = pl.BlockSpec(memory_space=pl.ANY)
    steps = SECTIONS * PARTS
    dma = pltpu.SemaphoreType.DMA
    rows, columns = c_partial.shape
    kept, scale = pl.pallas_call(
        functools.partial(kernel, n_row, n_col),
        out_shape=(
            jax.ShapeDtypeStruct((rows, columns), jnp.float32),
            jax.ShapeDtypeStruct((1, columns), jnp.float32),
        ),
        in_specs=[smem] * 5 + [hbm] * 3,
        out_specs=(hbm, pl.BlockSpec(memory_space=pltpu.VMEM)),
        scratch_shapes=[
            pltpu.VMEM((KA + 1, TILE, TILE), jnp.bfloat16),
            pltpu.VMEM((KA + 1, TILE, TILE), jnp.bfloat16),
            pltpu.VMEM((KB + 1, TILE, TILE), jnp.bfloat16),
            pltpu.VMEM((KB + 1, TILE, TILE), jnp.bfloat16),
            pltpu.VMEM((2 * SECTIONS, TILE), jnp.int32),
            pltpu.VMEM((SECTIONS, KB, TILE), jnp.int32),
            pltpu.VMEM((2 * SECTIONS, TILE), jnp.int32),
            pltpu.SMEM((2 * SECTIONS, TILE), jnp.int32),
            pltpu.VMEM((rows, columns), jnp.float32),
            pltpu.VMEM((n_row, 1, columns), jnp.float32),
            dma((2, steps)), dma((2, steps)),
            dma((steps,)), dma((steps,)), dma((steps,)), dma((steps,)),
            dma((1,)), dma((1,)), dma((3,)), dma((SECTIONS,)),
            dma((n_row,)), dma((n_row,)), dma((5,)),
        ],
        compiler_params=pltpu.CompilerParams(
            collective_id=0, has_side_effects=True, vmem_limit_bytes=32 * 1024 * 1024
        ),
        cost_estimate=pl.CostEstimate(
            flops=SECTIONS * 2 * rows * KA * TILE * columns, bytes_accessed=8 * rows * columns, transcendentals=0
        ),
    )(a_index, a_count, b_index, b_count, prune_mask, a_tiles, b_tiles, c_partial)
    return kept * scale


def solution(mesh):
    n_row, n_col = mesh.shape["row"], mesh.shape["col"]
    return jax.shard_map(
        functools.partial(local, n_row, n_col),
        mesh=mesh,
        in_specs=(
            P("row", "col", None, None, None, None),
            P("row", "col", None, None),
            P("row", "col", None),
            P("row", "col", None, None, None),
            P("row", "col", None),
            P("row", "col"),
            P("row", "col"),
            P("row", "col"),
        ),
        out_specs=P("row", "col"),
        check_vma=False,
    )
```

time: 163 us -> 134 us (0.82); the launches traced: 163 us -> 131 us
  Pallas kernels: 0 us -> 125 us
  waiting for transfers between devices: 70.7 us -> 0 us
  blocking collectives: 34.5 us -> 0 us
  local copies, waits for them, and re-layouts: 21.8 us -> 4.83 us
  matrix products: 16.5 us -> 0 us
  between operations: 14.2 us -> 0.72 us
  other arithmetic: 5.16 us -> 1.1 us
    pallas_call x0 -> x1, Pallas kernels: none -> 125 us  [local(): pl.pallas_call(functools.partial(kernel, n_row, n_col), out_shape=(jax.Sh...]
    psum x2 -> x0, waiting for transfers between devices: 70.6 us -> none  [spread(): return lax.psum(jnp.where(mine, array, jnp.zeros_like(array)), axis)]
    psum x3 -> x0, blocking collectives: 34.5 us -> none  [the longest x2 18.1 us: spread(): return lax.psum(jnp.where(mine, array, jnp.zeros_like(array)), axis)]
    reshape x4 -> x0, local copies, waits for them, and re-layouts: 18.7 us -> none  [the longest x2 17.1 us: section_product(): right_dense.reshape(W, NB, tile, tile).transpose(0, 2, 1, 3)]
    dot_general x6 -> x0, matrix products: 16.5 us -> none  [the longest x4 11.5 us: place_tiles(): jnp.einsum('ap,auv->puv', onehot, tiles, preferred_element_type=jnp.float32)]
    select_n x5 -> x0, other arithmetic: 4.04 us -> none  [the longest x4 3.97 us: spread(): return lax.psum(jnp.where(mine, array, jnp.zeros_like(array)), axis)]
    unnamed x18 -> x14, local copies, waits for them, and re-layouts: 1.62 us -> 4.83 us
  transfers between devices with their start and end apart: 2 -> 0, of which waited for: 2 -> 0; matrix products, arithmetic and copies ran while one was open for 17% -> 0% of each run, Pallas kernels for 0% -> 0%
where the time goes in v1:
time: 134 us; the launch traced here: 131 us
  Pallas kernels  125 us (93%)
  local copies, waits for them, and re-layouts  4.83 us (4%)
    pallas_call x1, Pallas kernels, local(): pl.pallas_call(functools.partial(kernel, n_row, n_col), out_shape=(jax.Sh...  125 us
    unnamed x14, local copies, waits for them, and re-layouts  4.83 us

profile of v1, /device:TPU:0, one launch (start us, length us, event | category | flops | bytes accessed | tf_op | source)
XLA Modules:
  0.0 131.3 jit_solution(14864800261692502616)
XLA Ops:
  0.0 0.0 copy-start.5
  0.0 0.0 copy-start.4
  0.7 0.0 copy-done.5
  0.7 0.0 copy-done.4
  0.7 0.0 copy-start
  0.7 1.2 copy-done
  1.9 0.0 copy-start.1
  1.9 1.2 copy-done.1
  3.2 0.0 copy-start.2
  3.2 1.0 copy-done.2
  4.2 0.0 copy-start.3
  4.2 0.7 copy-done.3
  4.9 0.0 copy-start.6
  4.9 0.7 copy-done.6
  5.5 124.7 %shard_map.82 = (f32[512,512]{1,0:T(8,128)S(1)}, f32[1,512]{1,0:T(1,128)S(1)}) custom-call(s32[1,1,2,16]{3,2,1,0:T(2,128)S(1)} %copy-done.4, s32[1,1,2]{2,1,0:T(1,128)S(1)} %copy-done.5, s32[1,1,16]{2,1,0:T(1,128)S(1)} %copy-done.6, s32[1,1]{1,0:T(1,128)S(6)} %copy.9.bc_ref, s32[4,4]{1,0:T(4,128)S(1)} %copy-done.3, ...), custom_call_target="tpu_custom_call" | custom-call | flops 2147483648 | bytes 2097152 | tf_op jit(solution)/shard_map/pallas_call | solution.py:387
  130.2 1.1 broadcast_multiply_fusion
Async XLA Ops:
  0.0 0.7 copy-start.5
  0.0 0.7 copy-start.4
  0.7 1.2 copy-start
  1.9 1.2 copy-start.1
  3.2 1.0 copy-start.2
  4.2 0.7 copy-start.3
  4.9 0.7 copy-start.6

commit v2 on v1

--- a/solution.py
+++ b/solution.py
@@ -45,9 +45,9 @@
 
 
 def kernel(
-    n_row, n_col, ai_ref, ac_ref, bi_ref, bc_ref, mask_ref, a_hbm, b_hbm, c_hbm,
+    n_row, n_col, ai_hbm, ac_hbm, bi_hbm, bc_hbm, mask_hbm, a_hbm, b_hbm, c_hbm,
     kept_hbm, scale_ref,
-    lt0, lt1, rt0, rt1, ma, mb, table, table_smem, acc, sums,
+    ai_ref, ac_ref, bi_ref, bc_ref, mask_ref, lt0, lt1, rt0, rt1, ma, mb, table, table_smem, acc, sums,
     a_send, a_recv, b_send, b_recv, sib_send, sib_recv, ma_send, ma_recv, mb_send, mb_recv,
     cs_send, cs_recv, loc,
 ):
@@ -61,6 +61,14 @@
 
     load_c = pltpu.make_async_copy(c_hbm, acc, loc.at[0])
     load_c.start()
+    small = [
+        pltpu.make_async_copy(source, target, loc.at[5 + i])
+        for i, (source, target) in enumerate(
+            ((ai_hbm, ai_ref), (ac_hbm, ac_ref), (bi_hbm, bi_ref), (bc_hbm, bc_ref), (mask_hbm, mask_ref))
+        )
+    ]
+    for copy in small:
+        copy.start()
 
     barrier = pltpu.get_barrier_semaphore()
     for d in range(1, n_row):
@@ -68,6 +76,12 @@
     for d in range(1, n_col):
         pl.semaphore_signal(barrier, inc=1, device_id=(row, (col + d) % n_col), device_id_type=MESH)
 
+    for s in range(SECTIONS):
+        lts[s][KA] = jnp.zeros((TILE, TILE), jnp.bfloat16)
+        rts[s][KB] = jnp.zeros((TILE, TILE), jnp.bfloat16)
+
+    for copy in small:
+        copy.wait()
     lane = lax.broadcasted_iota(jnp.int32, (1, TILE), 1)
 
     @pl.when(col == n_col - 1)
@@ -95,10 +109,6 @@
                 slot = jnp.where(b < count, bi_ref[0, 0, b], -1)
                 mb[s, b : b + 1, :] = jnp.full((1, TILE), slot, jnp.int32)
 
-    for s in range(SECTIONS):
-        lts[s][KA] = jnp.zeros((TILE, TILE), jnp.bfloat16)
-        rts[s][KB] = jnp.zeros((TILE, TILE), jnp.bfloat16)
-
     pl.semaphore_wait(barrier, n_row - 1 + n_col - 1)
 
     positions = [path_position(col, p, ny, nx) for p in range(2)]
@@ -107,8 +117,8 @@
     def next_col(p):
         return path_column((positions[p] + 1) % n_col, p, ny, nx)
 
-    def a_copy(p, i, from_hbm):
-        s, c = i // PARTS, i % PARTS
+    def a_copy(p, s, c, from_hbm):
+        i = s * PARTS + c
         tiles = pl.ds(p * (KA // 2) + c * STEP, STEP)
         return pltpu.make_async_remote_copy(
             src_ref=a_hbm.at[0, 0, s, tiles] if from_hbm else lts[s].at[tiles],
@@ -150,29 +160,22 @@
             device_id=(target, col), device_id_type=MESH,
         )
 
-    def b_tiles(i, k):
-        return pl.ds(k * (KB // 2) + (i % PARTS) * STEP, STEP)
-
-    def b_copy(i):
-        ref = rts[i // PARTS].at[b_tiles(i, core)]
-        return pltpu.make_async_remote_copy(
-            src_ref=ref, dst_ref=ref, send_sem=b_send.at[i], recv_sem=b_recv.at[i],
-            device_id=(below * 2 + core, col), device_id_type=MESH,
-        )
-
-    def sib_copy(i):
-        ref = rts[i // PARTS].at[b_tiles(i, core)]
-        return pltpu.make_async_remote_copy(
-            src_ref=ref, dst_ref=ref, send_sem=sib_send.at[i], recv_sem=sib_recv.at[i],
-            device_id=(sibling, col), device_id_type=MESH,
-        )
-
-    def sib_arrival(i):
-        ref = rts[i // PARTS].at[b_tiles(i, 1 - core)]
-        return pltpu.make_async_remote_copy(
-            src_ref=ref, dst_ref=ref, send_sem=sib_send.at[i], recv_sem=sib_recv.at[i],
-            device_id=(sibling, col), device_id_type=MESH,
-        )
+    def b_chain_copy(s, c, k, target, send, recv):
+        ref = rts[s].at[pl.ds(k * (KB // 2) + c * STEP, STEP)]
+        i = s * PARTS + c
+        return pltpu.make_async_remote_copy(
+            src_ref=ref, dst_ref=ref, send_sem=send.at[i], recv_sem=recv.at[i],
+            device_id=(target, col), device_id_type=MESH,
+        )
+
+    def b_copy(s, c):
+        return b_chain_copy(s, c, core, below * 2 + core, b_send, b_recv)
+
+    def sib_copy(s, c):
+        return b_chain_copy(s, c, core, sibling, sib_send, sib_recv)
+
+    def sib_arrival(s, c):
+        return b_chain_copy(s, c, 1 - core, sibling, sib_send, sib_recv)
 
     def b_local(s):
         return pltpu.make_async_copy(b_hbm.at[0, 0], rts[s].at[pl.ds(0, KB)], loc.at[3])
@@ -185,7 +188,7 @@
         ma_copy().start()
         for i in range(steps):
             for p in range(2):
-                a_copy(p, i, True).start()
+                a_copy(p, i // PARTS, i % PARTS, True).start()
         for s in range(SECTIONS):
             a_local(s).start()
 
@@ -202,36 +205,55 @@
             b_root_sibling(s).start()
             b_local(s).start()
 
-    @pl.when(positions[0] > 0)
-    def _():
-        ma_copy().wait_recv()
-
-        @pl.when(positions[0] < n_col - 1)
-        def _():
-            ma_copy().start()
-
-    def forward(i):
+    def forward(t):
         for p in range(2):
-
-            @pl.when(positions[p] > 0)
+            i = t - (positions[p] - 1)
+            passes = (positions[p] > 0) & (positions[p] < n_col - 1)
+            if p == 0:
+
+                @pl.when(passes & (i == 0))
+                def _():
+                    ma_copy().wait_recv()
+                    ma_copy().start()
+
+            for s in range(SECTIONS):
+                c = i - s * PARTS
+
+                @pl.when(passes & (c >= 0) & (c < PARTS))
+                def _(p=p, s=s, c=c):
+                    a_copy(p, s, c, False).wait_recv()
+                    a_copy(p, s, c, False).start()
+
+        i = t - (last_pair - 1 - pair)
+        for s in range(SECTIONS):
+            c = i - s * PARTS
+
+            @pl.when(in_chain & (c == 0))
+            def _(s=s):
+                mb_copy(s, below * 2 + core, s).wait_recv()
+
+                @pl.when(pair > 0)
+                def _():
+                    mb_copy(s, below * 2 + core, s).start()
+
+            @pl.when(in_chain & (c >= 0) & (c < PARTS))
+            def _(s=s, c=c):
+                b_copy(s, c).wait_recv()
+
+                @pl.when(pair > 0)
+                def _():
+                    b_copy(s, c).start()
+
+                sib_copy(s, c).start()
+
+    def section_ready(s):
+        for p in range(2):
+
+            @pl.when(positions[p] == n_col - 1)
             def _(p=p):
-                a_copy(p, i, False).wait_recv()
-
-                @pl.when(positions[p] < n_col - 1)
-                def _():
-                    a_copy(p, i, False).start()
-
-        @pl.when(in_chain)
-        def _():
-            b_copy(i).wait_recv()
-
-            @pl.when(pair > 0)
-            def _():
-                b_copy(i).start()
-
-            sib_copy(i).start()
-
-    def section_ready(s):
+                for c in range(PARTS):
+                    a_copy(p, s, c, False).wait_recv()
+
         @pl.when(is_left_root)
         def _():
             a_local(s).wait()
@@ -239,7 +261,7 @@
         @pl.when(in_chain)
         def _():
             for c in range(PARTS):
-                sib_arrival(s * PARTS + c).wait_recv()
+                sib_arrival(s, c).wait_recv()
 
         @pl.when(row == n_row - SECTIONS + s)
         def _():
@@ -249,27 +271,18 @@
         def _():
             b_root_sibling(s).wait_recv()
 
-    for s in range(SECTIONS):
-
-        @pl.when(in_chain)
-        def _(s=s):
-            mb_copy(s, below * 2 + core, s).wait_recv()
-
-            @pl.when(pair > 0)
-            def _():
-                mb_copy(s, below * 2 + core, s).start()
-
+    most = max(n_col - 3, last_pair - 1, 0)
+    for t in range(PARTS + most):
+        forward(t)
+
+    @pl.when(positions[0] == n_col - 1)
+    def _():
+        ma_copy().wait_recv()
+
+    for s in range(SECTIONS):
         @pl.when(row == n_row - 1 - s)
         def _(s=s):
             mb_copy(s, sibling, s).wait_recv()
-
-    row_id = lax.broadcasted_iota(jnp.int32, (KB, TILE), 0)
-    for s in range(SECTIONS):
-        hit = mb[s] == ma[s : s + 1, :]
-        table[s : s + 1, :] = jnp.min(jnp.where(hit, row_id, KB), axis=0, keepdims=True)
-    table[SECTIONS : 2 * SECTIONS, :] = ma[SECTIONS : 2 * SECTIONS, :]
-    to_smem = pltpu.make_async_copy(table, table_smem, loc.at[4])
-    to_smem.start()
 
     group = KA // PARTS
 
@@ -277,7 +290,7 @@
         left = jnp.concatenate(
             [
                 jnp.concatenate(
-                    [lts[s][table_smem[SECTIONS + s, m * KA + j * group + a]] for a in range(group)],
+                    [lts[s][table_smem[s, 1, m * KA + j * group + a]] for a in range(group)],
                     axis=1,
                 )
                 for m in range(MB)
@@ -287,7 +300,7 @@
         right = jnp.concatenate(
             [
                 jnp.concatenate(
-                    [rts[s][table_smem[s, (j * group + a) * NB + n]] for n in range(NB)], axis=1
+                    [rts[s][table_smem[s, 0, (j * group + a) * NB + n]] for n in range(NB)], axis=1
                 )
                 for a in range(group)
             ],
@@ -295,15 +308,22 @@
         )
         acc[...] += jnp.dot(left, right, preferred_element_type=jnp.float32)
 
-    for i in range(PARTS):
-        forward(i)
-    to_smem.wait()
+    row_id = lax.broadcasted_iota(jnp.int32, (KB, TILE), 0)
+
+    def make_table(s):
+        table[0:1, :] = jnp.min(jnp.where(mb[s] == ma[s : s + 1, :], row_id, KB), axis=0, keepdims=True)
+        table[1:2, :] = ma[SECTIONS + s : SECTIONS + s + 1, :]
+        to_smem = pltpu.make_async_copy(table, table_smem.at[s], loc.at[4])
+        to_smem.start()
+        to_smem.wait()
+
     load_c.wait()
     for s in range(SECTIONS):
         section_ready(s)
+        make_table(s)
         for j in range(PARTS):
             if s + 1 < SECTIONS:
-                forward((s + 1) * PARTS + j)
+                forward(PARTS + most + j)
             product(s, j)
 
     partial = jnp.zeros((1, NB * TILE), jnp.float32)
@@ -345,7 +365,7 @@
         @pl.when(positions[p] < n_col - 1)
         def _(p=p):
             for i in range(steps):
-                a_copy(p, i, False).wait_send()
+                a_copy(p, i // PARTS, i % PARTS, False).wait_send()
 
     @pl.when(positions[0] < n_col - 1)
     def _():
@@ -354,12 +374,12 @@
     @pl.when(in_chain)
     def _():
         for i in range(steps):
-            sib_copy(i).wait_send()
+            sib_copy(i // PARTS, i % PARTS).wait_send()
 
         @pl.when(pair > 0)
         def _():
             for i in range(steps):
-                b_copy(i).wait_send()
+                b_copy(i // PARTS, i % PARTS).wait_send()
             for s in range(SECTIONS):
                 mb_copy(s, below * 2 + core, s).wait_send()
 
@@ -379,8 +399,7 @@
 
 
 def local(n_row, n_col, a_tiles, a_index, a_count, b_tiles, b_index, b_count, c_partial, prune_mask):
-    smem = pl.BlockSpec(memory_space=pltpu.SMEM)
-    hbm = pl.BlockSpec(memory_space=pl.ANY)
+    hbm = pl.BlockSpec(memory_space=pltpu.HBM)
     steps = SECTIONS * PARTS
     dma = pltpu.SemaphoreType.DMA
     rows, columns = c_partial.shape
@@ -390,26 +409,31 @@
             jax.ShapeDtypeStruct((rows, columns), jnp.float32),
             jax.ShapeDtypeStruct((1, columns), jnp.float32),
         ),
-        in_specs=[smem] * 5 + [hbm] * 3,
-        out_specs=(hbm, pl.BlockSpec(memory_space=pltpu.VMEM)),
+        in_specs=[hbm] * 8,
+        out_specs=(pl.BlockSpec(memory_space=pl.ANY), pl.BlockSpec(memory_space=pltpu.VMEM)),
         scratch_shapes=[
+            pltpu.SMEM(a_index.shape, jnp.int32),
+            pltpu.SMEM(a_count.shape, jnp.int32),
+            pltpu.SMEM(b_index.shape, jnp.int32),
+            pltpu.SMEM(b_count.shape, jnp.int32),
+            pltpu.SMEM(prune_mask.shape, jnp.int32),
             pltpu.VMEM((KA + 1, TILE, TILE), jnp.bfloat16),
             pltpu.VMEM((KA + 1, TILE, TILE), jnp.bfloat16),
             pltpu.VMEM((KB + 1, TILE, TILE), jnp.bfloat16),
             pltpu.VMEM((KB + 1, TILE, TILE), jnp.bfloat16),
             pltpu.VMEM((2 * SECTIONS, TILE), jnp.int32),
             pltpu.VMEM((SECTIONS, KB, TILE), jnp.int32),
-            pltpu.VMEM((2 * SECTIONS, TILE), jnp.int32),
-            pltpu.SMEM((2 * SECTIONS, TILE), jnp.int32),
+            pltpu.VMEM((2, TILE), jnp.int32),
+            pltpu.SMEM((SECTIONS, 2, TILE), jnp.int32),
             pltpu.VMEM((rows, columns), jnp.float32),
             pltpu.VMEM((n_row, 1, columns), jnp.float32),
             dma((2, steps)), dma((2, steps)),
             dma((steps,)), dma((steps,)), dma((steps,)), dma((steps,)),
             dma((1,)), dma((1,)), dma((3,)), dma((SECTIONS,)),
-            dma((n_row,)), dma((n_row,)), dma((5,)),
+            dma((n_row,)), dma((n_row,)), dma((10,)),
         ],
         compiler_params=pltpu.CompilerParams(
-            collective_id=0, has_side_effects=True, vmem_limit_bytes=32 * 1024 * 1024
+            collective_id=0, has_side_effects=True, vmem_limit_bytes=62 * 1024 * 1024
         ),
         cost_estimate=pl.CostEstimate(
             flops=SECTIONS * 2 * rows * KA * TILE * columns, bytes_accessed=8 * rows * columns, transcendentals=0

time: 134 us -> 42.7 us (0.32); the launches traced: 131 us -> 42.4 us
  Pallas kernels: 125 us -> 38.7 us
  local copies, waits for them, and re-layouts: 4.83 us -> 0.65 us
    pallas_call x1, Pallas kernels: 125 us -> 38.7 us  [local(): pl.pallas_call(functools.partial(kernel, n_row, n_col), out_shape=(jax.Sh...]
    unnamed x14 -> x2, local copies, waits for them, and re-layouts: 4.83 us -> 0.65 us
where the time goes in v2:
time: 42.7 us; the launch traced here: 42.4 us
  Pallas kernels  38.7 us (91%)
  other arithmetic  2.33 us (5%)
  between operations  0.67 us (2%)
  local copies, waits for them, and re-layouts  0.65 us (2%)
    pallas_call x1, Pallas kernels, local(): pl.pallas_call(functools.partial(kernel, n_row, n_col), out_shape=(jax.Sh...  38.7 us
    mul x1, other arithmetic, local(): return kept * scale  2.33 us

profile of v2, /device:TPU:0, one launch (start us, length us, event | category | flops | bytes accessed | tf_op | source)
XLA Modules:
  0.0 42.4 jit_solution(3034323521485706533)
XLA Ops:
  0.7 38.7 %shard_map.82 = (f32[512,512]{1,0:T(8,128)}, f32[1,512]{1,0:T(1,128)}) custom-call(s32[1,1,2,16]{3,2,1,0:T(2,128)} %ai_hbm.1, s32[1,1,2]{2,1,0:T(1,128)} %ac_hbm.1, s32[1,1,16]{2,1,0:T(1,128)} %bi_hbm.1, s32[1,1]{1,0:T(1,128)S(6)} %copy.9.bc_hbm, s32[4,4]{1,0:T(4,128)} %mask_hbm.1, bf16[1,1,2,16,128,128]{5,4,3,2,1,0:T(8,128)(2,1)} %a_hbm.1, ...), custom_call_target="tpu_custom_call" | custom-call | flops 2147483648 | bytes 2097152 | tf_op jit(solution)/shard_map/pallas_call | solution.py:406
  39.4 0.0 copy-start
  39.4 0.6 %copy-done = f32[1,512]{1,0:T(1,128)S(1)} copy-done((f32[1,512]{1,0:T(1,128)S(1)}, f32[1,512]{1,0:T(1,128)}, u32[]{:S(2)}) %copy-start) | copy-done | bytes 2072
  40.1 2.3 %broadcast_multiply_fusion = f32[512,512]{1,0:T(8,128)} fusion(f32[512,512]{1,0:T(8,128)} %get-tuple-element.7, f32[512]{0:T(512)S(1)} %bitcast.1), kind=kLoop, calls=%fused_computation | loop fusion | flops 262144 | bytes 2099200 | tf_op jit(solution)/shard_map/mul | solution.py:442
Async XLA Ops:
  39.4 0.7 %copy-start = (f32[1,512]{1,0:T(1,128)S(1)}, f32[1,512]{1,0:T(1,128)}, u32[]{:S(2)}) copy-start(f32[1,512]{1,0:T(1,128)} %get-tuple-element.8) | copy-start | bytes 6148

commit v3 on v2

--- a/solution.py
+++ b/solution.py
@@ -16,6 +16,8 @@
 TILE = 128
 STEP = 2
 PARTS = KA // 2 // STEP
+WINDOW = 2
+LAG = 2
 MESH = pl.DeviceIdType.MESH
 
 
@@ -186,11 +188,6 @@
     @pl.when(is_left_root)
     def _():
         ma_copy().start()
-        for i in range(steps):
-            for p in range(2):
-                a_copy(p, i // PARTS, i % PARTS, True).start()
-        for s in range(SECTIONS):
-            a_local(s).start()
 
     for s in range(SECTIONS):
 
@@ -199,15 +196,41 @@
             for k in range(2):
                 mb_copy(s, below * 2 + k, k).start()
             mb_copy(s, sibling, 2).start()
-            for c in range(PARTS):
+
+    def forward(t):
+        if t < steps:
+
+            @pl.when(is_left_root)
+            def _():
+                for p in range(2):
+                    if t >= WINDOW:
+                        a_copy(p, (t - WINDOW) // PARTS, (t - WINDOW) % PARTS, True).wait_send()
+                    a_copy(p, t // PARTS, t % PARTS, True).start()
+
+            @pl.when(row == n_row - SECTIONS + t // PARTS)
+            def _():
+                s, c = t // PARTS, t % PARTS
                 for k in range(2):
+                    if c >= WINDOW:
+                        b_root_copy(s, k, c - WINDOW).wait_send()
                     b_root_copy(s, k, c).start()
-            b_root_sibling(s).start()
-            b_local(s).start()
-
-    def forward(t):
+
+        if t == 0:
+
+            @pl.when(is_left_root)
+            def _():
+                for s in range(SECTIONS):
+                    a_local(s).start()
+
+            for s in range(SECTIONS):
+
+                @pl.when(row == n_row - SECTIONS + s)
+                def _(s=s):
+                    b_root_sibling(s).start()
+                    b_local(s).start()
+
         for p in range(2):
-            i = t - (positions[p] - 1)
+            i = t - LAG * (positions[p] - 1)
             passes = (positions[p] > 0) & (positions[p] < n_col - 1)
             if p == 0:
 
@@ -224,7 +247,7 @@
                     a_copy(p, s, c, False).wait_recv()
                     a_copy(p, s, c, False).start()
 
-        i = t - (last_pair - 1 - pair)
+        i = t - LAG * (last_pair - 1 - pair)
         for s in range(SECTIONS):
             c = i - s * PARTS
 
@@ -271,7 +294,7 @@
         def _():
             b_root_sibling(s).wait_recv()
 
-    most = max(n_col - 3, last_pair - 1, 0)
+    most = LAG * max(n_col - 3, last_pair - 1, 0)
     for t in range(PARTS + most):
         forward(t)
 
@@ -362,10 +385,15 @@
         cs_copy((row + d) % n_row, row).wait_send()
     for p in range(2):
 
-        @pl.when(positions[p] < n_col - 1)
+        @pl.when((positions[p] > 0) & (positions[p] < n_col - 1))
         def _(p=p):
             for i in range(steps):
                 a_copy(p, i // PARTS, i % PARTS, False).wait_send()
+
+        @pl.when(is_left_root)
+        def _(p=p):
+            for i in range(steps - WINDOW, steps):
+                a_copy(p, i // PARTS, i % PARTS, True).wait_send()
 
     @pl.when(positions[0] < n_col - 1)
     def _():
@@ -390,7 +418,7 @@
             for k in range(2):
                 mb_copy(s, below * 2 + k, k).wait_send()
             mb_copy(s, sibling, 2).wait_send()
-            for c in range(PARTS):
+            for c in range(PARTS - WINDOW, PARTS):
                 for k in range(2):
                     b_root_copy(s, k, c).wait_send()
             b_root_sibling(s).wait_send()

time: 42.7 us -> 39.7 us (0.930)
  Pallas kernels: 38.7 us -> 35.8 us
    pallas_call x1, Pallas kernels: 38.7 us -> 35.8 us  [local(): pl.pallas_call(functools.partial(kernel, n_row, n_col), out_shape=(jax.Sh...]
where the time goes in v3:
time: 39.7 us; the launch traced here: 39.5 us
  Pallas kernels  35.8 us (90%)
  other arithmetic  2.33 us (6%)
  between operations  0.67 us (2%)
  local copies, waits for them, and re-layouts  0.65 us (2%)
    pallas_call x1, Pallas kernels, local(): pl.pallas_call(functools.partial(kernel, n_row, n_col), out_shape=(jax.Sh...  35.8 us
    mul x1, other arithmetic, local(): return kept * scale  2.33 us

profile of v3, /device:TPU:0, one launch (start us, length us, event | category | flops | bytes accessed | tf_op | source)
XLA Modules:
  0.0 39.5 jit_solution(12002520374373069144)
XLA Ops:
  0.7 35.8 %shard_map.82 = (f32[512,512]{1,0:T(8,128)}, f32[1,512]{1,0:T(1,128)}) custom-call(s32[1,1,2,16]{3,2,1,0:T(2,128)} %ai_hbm.1, s32[1,1,2]{2,1,0:T(1,128)} %ac_hbm.1, s32[1,1,16]{2,1,0:T(1,128)} %bi_hbm.1, s32[1,1]{1,0:T(1,128)S(6)} %copy.9.bc_hbm, s32[4,4]{1,0:T(4,128)} %mask_hbm.1, bf16[1,1,2,16,128,128]{5,4,3,2,1,0:T(8,128)(2,1)} %a_hbm.1, ...), custom_call_target="tpu_custom_call" | custom-call | flops 2147483648 | bytes 2097152 | tf_op jit(solution)/shard_map/pallas_call | solution.py:434
  36.5 0.0 copy-start
  36.5 0.6 %copy-done = f32[1,512]{1,0:T(1,128)S(1)} copy-done((f32[1,512]{1,0:T(1,128)S(1)}, f32[1,512]{1,0:T(1,128)}, u32[]{:S(2)}) %copy-start) | copy-done | bytes 2072
  37.1 2.3 %broadcast_multiply_fusion = f32[512,512]{1,0:T(8,128)} fusion(f32[512,512]{1,0:T(8,128)} %get-tuple-element.7, f32[512]{0:T(512)S(1)} %bitcast.1), kind=kLoop, calls=%fused_computation | loop fusion | flops 262144 | bytes 2099200 | tf_op jit(solution)/shard_map/mul | solution.py:470
Async XLA Ops:
  36.5 0.7 %copy-start = (f32[1,512]{1,0:T(1,128)S(1)}, f32[1,512]{1,0:T(1,128)}, u32[]{:S(2)}) copy-start(f32[1,512]{1,0:T(1,128)} %get-tuple-element.8) | copy-start | bytes 6148

commit v4 on v3

--- a/solution.py
+++ b/solution.py
@@ -48,8 +48,8 @@
 
 def kernel(
     n_row, n_col, ai_hbm, ac_hbm, bi_hbm, bc_hbm, mask_hbm, a_hbm, b_hbm, c_hbm,
-    kept_hbm, scale_ref,
-    ai_ref, ac_ref, bi_ref, bc_ref, mask_ref, lt0, lt1, rt0, rt1, ma, mb, table, table_smem, acc, sums,
+    acc, scale_ref,
+    ai_ref, ac_ref, bi_ref, bc_ref, mask_ref, lt0, lt1, rt0, rt1, ma, mb, table, table_smem, sums,
     a_send, a_recv, b_send, b_recv, sib_send, sib_recv, ma_send, ma_recv, mb_send, mb_recv,
     cs_send, cs_recv, loc,
 ):
@@ -81,6 +81,116 @@
     for s in range(SECTIONS):
         lts[s][KA] = jnp.zeros((TILE, TILE), jnp.bfloat16)
         rts[s][KB] = jnp.zeros((TILE, TILE), jnp.bfloat16)
+
+    pl.semaphore_wait(barrier, n_row - 1 + n_col - 1)
+
+    positions = [path_position(col, p, ny, nx) for p in range(2)]
+    is_left_root = col == n_col - 1
+
+    def next_col(p):
+        return path_column((positions[p] + 1) % n_col, p, ny, nx)
+
+    def a_copy(p, s, c, from_hbm):
+        i = s * PARTS + c
+        tiles = pl.ds(p * (KA // 2) + c * STEP, STEP)
+        return pltpu.make_async_remote_copy(
+            src_ref=a_hbm.at[0, 0, s, tiles] if from_hbm else lts[s].at[tiles],
+            dst_ref=lts[s].at[tiles],
+            send_sem=a_send.at[p, i], recv_sem=a_recv.at[p, i],
+            device_id=(row, next_col(p)), device_id_type=MESH,
+        )
+
+    def ma_copy():
+        return pltpu.make_async_remote_copy(
+            src_ref=ma, dst_ref=ma, send_sem=ma_send.at[0], recv_sem=ma_recv.at[0],
+            device_id=(row, next_col(0)), device_id_type=MESH,
+        )
+
+    def a_local(s):
+        return pltpu.make_async_copy(a_hbm.at[0, 0, s], lts[s].at[pl.ds(0, KA)], loc.at[1 + s])
+
+    below = (pair - 1 + last_pair + 1) % (last_pair + 1)
+    sibling = pair * 2 + 1 - core
+
+    def b_root_copy(s, k, c):
+        tiles = pl.ds(k * (KB // 2) + c * STEP, STEP)
+        return pltpu.make_async_remote_copy(
+            src_ref=b_hbm.at[0, 0, tiles], dst_ref=rts[s].at[tiles],
+            send_sem=b_send.at[k * PARTS + c], recv_sem=b_recv.at[s * PARTS + c],
+            device_id=(below * 2 + k, col), device_id_type=MESH,
+        )
+
+    def b_root_sibling(s):
+        return pltpu.make_async_remote_copy(
+            src_ref=b_hbm.at[0, 0], dst_ref=rts[s].at[pl.ds(0, KB)],
+            send_sem=sib_send.at[0], recv_sem=sib_recv.at[s * PARTS],
+            device_id=(sibling, col), device_id_type=MESH,
+        )
+
+    def mb_copy(s, target, sem):
+        return pltpu.make_async_remote_copy(
+            src_ref=mb.at[s], dst_ref=mb.at[s], send_sem=mb_send.at[sem], recv_sem=mb_recv.at[s],
+            device_id=(target, col), device_id_type=MESH,
+        )
+
+    def b_chain_copy(s, c, k, target, send, recv):
+        ref = rts[s].at[pl.ds(k * (KB // 2) + c * STEP, STEP)]
+        i = s * PARTS + c
+        return pltpu.make_async_remote_copy(
+            src_ref=ref, dst_ref=ref, send_sem=send.at[i], recv_sem=recv.at[i],
+            device_id=(target, col), device_id_type=MESH,
+        )
+
+    def b_copy(s, c):
+        return b_chain_copy(s, c, core, below * 2 + core, b_send, b_recv)
+
+    def sib_copy(s, c):
+        return b_chain_copy(s, c, core, sibling, sib_send, sib_recv)
+
+    def sib_arrival(s, c):
+        return b_chain_copy(s, c, 1 - core, sibling, sib_send, sib_recv)
+
+    def b_local(s):
+        return pltpu.make_async_copy(b_hbm.at[0, 0], rts[s].at[pl.ds(0, KB)], loc.at[3])
+
+    steps = SECTIONS * PARTS
+    in_chain = pair < last_pair
+
+    def root_start(t):
+        if t < steps:
+
+            @pl.when(is_left_root)
+            def _():
+                for p in range(2):
+                    if t >= WINDOW:
+                        a_copy(p, (t - WINDOW) // PARTS, (t - WINDOW) % PARTS, True).wait_send()
+                    a_copy(p, t // PARTS, t % PARTS, True).start()
+
+        for s in range(SECTIONS):
+            c = t - WINDOW * s
+            if 0 <= c < PARTS:
+
+                @pl.when(row == n_row - SECTIONS + s)
+                def _(s=s, c=c):
+                    for k in range(2):
+                        if c >= WINDOW:
+                            b_root_copy(s, k, c - WINDOW).wait_send()
+                        b_root_copy(s, k, c).start()
+
+    for t in range(WINDOW):
+        root_start(t)
+
+    @pl.when(is_left_root)
+    def _():
+        for s in range(SECTIONS):
+            a_local(s).start()
+
+    for s in range(SECTIONS):
+
+        @pl.when(row == n_row - SECTIONS + s)
+        def _(s=s):
+            b_root_sibling(s).start()
+            b_local(s).start()
 
     for copy in small:
         copy.wait()
@@ -111,80 +221,6 @@
                 slot = jnp.where(b < count, bi_ref[0, 0, b], -1)
                 mb[s, b : b + 1, :] = jnp.full((1, TILE), slot, jnp.int32)
 
-    pl.semaphore_wait(barrier, n_row - 1 + n_col - 1)
-
-    positions = [path_position(col, p, ny, nx) for p in range(2)]
-    is_left_root = col == n_col - 1
-
-    def next_col(p):
-        return path_column((positions[p] + 1) % n_col, p, ny, nx)
-
-    def a_copy(p, s, c, from_hbm):
-        i = s * PARTS + c
-        tiles = pl.ds(p * (KA // 2) + c * STEP, STEP)
-        return pltpu.make_async_remote_copy(
-            src_ref=a_hbm.at[0, 0, s, tiles] if from_hbm else lts[s].at[tiles],
-            dst_ref=lts[s].at[tiles],
-            send_sem=a_send.at[p, i], recv_sem=a_recv.at[p, i],
-            device_id=(row, next_col(p)), device_id_type=MESH,
-        )
-
-    def ma_copy():
-        return pltpu.make_async_remote_copy(
-            src_ref=ma, dst_ref=ma, send_sem=ma_send.at[0], recv_sem=ma_recv.at[0],
-            device_id=(row, next_col(0)), device_id_type=MESH,
-        )
-
-    def a_local(s):
-        return pltpu.make_async_copy(a_hbm.at[0, 0, s], lts[s].at[pl.ds(0, KA)], loc.at[1 + s])
-
-    below = (pair - 1 + last_pair + 1) % (last_pair + 1)
-    sibling = pair * 2 + 1 - core
-
-    def b_root_copy(s, k, c):
-        tiles = pl.ds(k * (KB // 2) + c * STEP, STEP)
-        return pltpu.make_async_remote_copy(
-            src_ref=b_hbm.at[0, 0, tiles], dst_ref=rts[s].at[tiles],
-            send_sem=b_send.at[k * PARTS + c], recv_sem=b_recv.at[s * PARTS + c],
-            device_id=(below * 2 + k, col), device_id_type=MESH,
-        )
-
-    def b_root_sibling(s):
-        return pltpu.make_async_remote_copy(
-            src_ref=b_hbm.at[0, 0], dst_ref=rts[s].at[pl.ds(0, KB)],
-            send_sem=sib_send.at[0], recv_sem=sib_recv.at[s * PARTS],
-            device_id=(sibling, col), device_id_type=MESH,
-        )
-
-    def mb_copy(s, target, sem):
-        return pltpu.make_async_remote_copy(
-            src_ref=mb.at[s], dst_ref=mb.at[s], send_sem=mb_send.at[sem], recv_sem=mb_recv.at[s],
-            device_id=(target, col), device_id_type=MESH,
-        )
-
-    def b_chain_copy(s, c, k, target, send, recv):
-        ref = rts[s].at[pl.ds(k * (KB // 2) + c * STEP, STEP)]
-        i = s * PARTS + c
-        return pltpu.make_async_remote_copy(
-            src_ref=ref, dst_ref=ref, send_sem=send.at[i], recv_sem=recv.at[i],
-            device_id=(target, col), device_id_type=MESH,
-        )
-
-    def b_copy(s, c):
-        return b_chain_copy(s, c, core, below * 2 + core, b_send, b_recv)
-
-    def sib_copy(s, c):
-        return b_chain_copy(s, c, core, sibling, sib_send, sib_recv)
-
-    def sib_arrival(s, c):
-        return b_chain_copy(s, c, 1 - core, sibling, sib_send, sib_recv)
-
-    def b_local(s):
-        return pltpu.make_async_copy(b_hbm.at[0, 0], rts[s].at[pl.ds(0, KB)], loc.at[3])
-
-    steps = SECTIONS * PARTS
-    in_chain = pair < last_pair
-
     @pl.when(is_left_root)
     def _():
         ma_copy().start()
@@ -198,47 +234,10 @@
             mb_copy(s, sibling, 2).start()
 
     def forward(t):
-        if t < steps:
-
-            @pl.when(is_left_root)
-            def _():
-                for p in range(2):
-                    if t >= WINDOW:
-                        a_copy(p, (t - WINDOW) // PARTS, (t - WINDOW) % PARTS, True).wait_send()
-                    a_copy(p, t // PARTS, t % PARTS, True).start()
-
-            @pl.when(row == n_row - SECTIONS + t // PARTS)
-            def _():
-                s, c = t // PARTS, t % PARTS
-                for k in range(2):
-                    if c >= WINDOW:
-                        b_root_copy(s, k, c - WINDOW).wait_send()
-                    b_root_copy(s, k, c).start()
-
-        if t == 0:
-
-            @pl.when(is_left_root)
-            def _():
-                for s in range(SECTIONS):
-                    a_local(s).start()
-
-            for s in range(SECTIONS):
-
-                @pl.when(row == n_row - SECTIONS + s)
-                def _(s=s):
-                    b_root_sibling(s).start()
-                    b_local(s).start()
-
+        root_start(t + WINDOW)
         for p in range(2):
             i = t - LAG * (positions[p] - 1)
             passes = (positions[p] > 0) & (positions[p] < n_col - 1)
-            if p == 0:
-
-                @pl.when(passes & (i == 0))
-                def _():
-                    ma_copy().wait_recv()
-                    ma_copy().start()
-
             for s in range(SECTIONS):
                 c = i - s * PARTS
 
@@ -247,27 +246,34 @@
                     a_copy(p, s, c, False).wait_recv()
                     a_copy(p, s, c, False).start()
 
+            if p == 0:
+
+                @pl.when(passes & (i == 1))
+                def _():
+                    ma_copy().wait_recv()
+                    ma_copy().start()
+
         i = t - LAG * (last_pair - 1 - pair)
         for s in range(SECTIONS):
             c = i - s * PARTS
 
-            @pl.when(in_chain & (c == 0))
+            @pl.when(in_chain & (c >= 0) & (c < PARTS))
+            def _(s=s, c=c):
+                b_copy(s, c).wait_recv()
+
+                @pl.when(pair > 0)
+                def _():
+                    b_copy(s, c).start()
+
+                sib_copy(s, c).start()
+
+            @pl.when(in_chain & (c == 1))
             def _(s=s):
                 mb_copy(s, below * 2 + core, s).wait_recv()
 
                 @pl.when(pair > 0)
                 def _():
                     mb_copy(s, below * 2 + core, s).start()
-
-            @pl.when(in_chain & (c >= 0) & (c < PARTS))
-            def _(s=s, c=c):
-                b_copy(s, c).wait_recv()
-
-                @pl.when(pair > 0)
-                def _():
-                    b_copy(s, c).start()
-
-                sib_copy(s, c).start()
 
     def section_ready(s):
         for p in range(2):
@@ -362,9 +368,6 @@
         kept = block * block * keep
         acc[m * TILE : (m + 1) * TILE, :] = kept
         partial = partial + jnp.sum(kept, axis=0, keepdims=True)
-    store = pltpu.make_async_copy(acc, kept_hbm, loc.at[0])
-    store.start()
-
     sums[row] = partial
 
     def cs_copy(target, slot):
@@ -423,8 +426,6 @@
                     b_root_copy(s, k, c).wait_send()
             b_root_sibling(s).wait_send()
 
-    store.wait()
-
 
 def local(n_row, n_col, a_tiles, a_index, a_count, b_tiles, b_index, b_count, c_partial, prune_mask):
     hbm = pl.BlockSpec(memory_space=pltpu.HBM)
@@ -434,11 +435,11 @@
     kept, scale = pl.pallas_call(
         functools.partial(kernel, n_row, n_col),
         out_shape=(
-            jax.ShapeDtypeStruct((rows, columns), jnp.float32),
-            jax.ShapeDtypeStruct((1, columns), jnp.float32),
+            pltpu.VMEM((rows, columns), jnp.float32),
+            pltpu.VMEM((1, columns), jnp.float32),
         ),
         in_specs=[hbm] * 8,
-        out_specs=(pl.BlockSpec(memory_space=pl.ANY), pl.BlockSpec(memory_space=pltpu.VMEM)),
+        out_specs=(pl.BlockSpec(memory_space=pltpu.VMEM), pl.BlockSpec(memory_space=pltpu.VMEM)),
         scratch_shapes=[
             pltpu.SMEM(a_index.shape, jnp.int32),
             pltpu.SMEM(a_count.shape, jnp.int32),
@@ -453,7 +454,6 @@
             pltpu.VMEM((SECTIONS, KB, TILE), jnp.int32),
             pltpu.VMEM((2, TILE), jnp.int32),
             pltpu.SMEM((SECTIONS, 2, TILE), jnp.int32),
-            pltpu.VMEM((rows, columns), jnp.float32),
             pltpu.VMEM((n_row, 1, columns), jnp.float32),
             dma((2, steps)), dma((2, steps)),
             dma((steps,)), dma((steps,)), dma((steps,)), dma((steps,)),
@@ -461,7 +461,7 @@
             dma((n_row,)), dma((n_row,)), dma((10,)),
         ],
         compiler_params=pltpu.CompilerParams(
-            collective_id=0, has_side_effects=True, vmem_limit_bytes=62 * 1024 * 1024
+            collective_id=0, has_side_effects=True, vmem_limit_bytes=60 * 1024 * 1024
         ),
         cost_estimate=pl.CostEstimate(
             flops=SECTIONS * 2 * rows * KA * TILE * columns, bytes_accessed=8 * rows * columns, transcendentals=0

time: 39.7 us -> 38 us (0.957)
  other arithmetic: 2.33 us -> 1.1 us
  local copies, waits for them, and re-layouts: 0.65 us -> 0 us
    mul x1, other arithmetic: 2.33 us -> 1.1 us  [local(): return kept * scale]
    unnamed x2 -> x0, local copies, waits for them, and re-layouts: 0.65 us -> none
where the time goes in v4:
time: 38 us; the launch traced here: 37.9 us
  Pallas kernels  36.1 us (95%)
  other arithmetic  1.1 us (3%)
  between operations  0.66 us (2%)
    pallas_call x1, Pallas kernels, local(): pl.pallas_call(functools.partial(kernel, n_row, n_col), out_shape=(pltpu....  36.1 us
    mul x1, other arithmetic, local(): return kept * scale  1.1 us

profile of v4, /device:TPU:0, one launch (start us, length us, event | category | flops | bytes accessed | tf_op | source)
XLA Modules:
  0.0 37.9 jit_solution(9922715862385188392)
XLA Ops:
  0.7 36.1 %shard_map.82 = (f32[512,512]{1,0:T(8,128)S(1)}, f32[1,512]{1,0:T(1,128)S(1)}) custom-call(s32[1,1,2,16]{3,2,1,0:T(2,128)} %ai_hbm.1, s32[1,1,2]{2,1,0:T(1,128)} %ac_hbm.1, s32[1,1,16]{2,1,0:T(1,128)} %bi_hbm.1, s32[1,1]{1,0:T(1,128)S(6)} %copy.9.bc_hbm, s32[4,4]{1,0:T(4,128)} %mask_hbm.1, bf16[1,1,2,16,128,128]{5,4,3,2,1,0:T(8,128)(2,1)} %a_hbm.1, ...), custom_call_target="tpu_custom_call" | custom-call | flops 2147483648 | bytes 2097152 | tf_op jit(solution)/shard_map/pallas_call | solution.py:435
  36.8 1.1 %broadcast_multiply_fusion = f32[512,512]{1,0:T(8,128)} fusion(f32[512,512]{1,0:T(8,128)S(1)} %get-tuple-element.7, f32[512]{0:T(512)S(1)} %bitcast.1), kind=kLoop, calls=%fused_computation | loop fusion | flops 262144 | bytes 2099200 | tf_op jit(solution)/shard_map/mul | solution.py:470

commit v5 on v4

--- a/solution.py
+++ b/solution.py
@@ -14,10 +14,10 @@
 KB = 16
 SECTIONS = 2
 TILE = 128
-STEP = 2
+STEP = 1
 PARTS = KA // 2 // STEP
-WINDOW = 2
-LAG = 2
+WINDOW = 3
+LAG = 3
 MESH = pl.DeviceIdType.MESH
 
 
@@ -167,7 +167,7 @@
                     a_copy(p, t // PARTS, t % PARTS, True).start()
 
         for s in range(SECTIONS):
-            c = t - WINDOW * s
+            c = t - PARTS // 2 * s
             if 0 <= c < PARTS:
 
                 @pl.when(row == n_row - SECTIONS + s)
@@ -309,11 +309,14 @@
         ma_copy().wait_recv()
 
     for s in range(SECTIONS):
+
         @pl.when(row == n_row - 1 - s)
         def _(s=s):
             mb_copy(s, sibling, s).wait_recv()
 
-    group = KA // PARTS
+    group = 4
+    products = KA // group
+    slots = PARTS // products
 
     def product(s, j):
         left = jnp.concatenate(
@@ -350,9 +353,10 @@
     for s in range(SECTIONS):
         section_ready(s)
         make_table(s)
-        for j in range(PARTS):
+        for j in range(products):
             if s + 1 < SECTIONS:
-                forward(PARTS + most + j)
+                for t in range(slots):
+                    forward(PARTS + most + j * slots + t)
             product(s, j)
 
     partial = jnp.zeros((1, NB * TILE), jnp.float32)

time: 38 us -> 38.3 us (level)
  no operation moved by 1% of the time
where the time goes in v5:
time: 38.3 us; the launch traced here: 38.1 us
  Pallas kernels  36.4 us (95%)
  other arithmetic  1.1 us (3%)
  between operations  0.66 us (2%)
    pallas_call x1, Pallas kernels, local(): pl.pallas_call(functools.partial(kernel, n_row, n_col), out_shape=(pltpu....  36.4 us
    mul x1, other arithmetic, local(): return kept * scale  1.1 us

profile of v5, /device:TPU:0, one launch (start us, length us, event | category | flops | bytes accessed | tf_op | source)
XLA Modules:
  0.0 38.1 jit_solution(18119569273595405951)
XLA Ops:
  0.7 36.4 %shard_map.82 = (f32[512,512]{1,0:T(8,128)S(1)}, f32[1,512]{1,0:T(1,128)S(1)}) custom-call(s32[1,1,2,16]{3,2,1,0:T(2,128)} %ai_hbm.1, s32[1,1,2]{2,1,0:T(1,128)} %ac_hbm.1, s32[1,1,16]{2,1,0:T(1,128)} %bi_hbm.1, s32[1,1]{1,0:T(1,128)S(6)} %copy.9.bc_hbm, s32[4,4]{1,0:T(4,128)} %mask_hbm.1, bf16[1,1,2,16,128,128]{5,4,3,2,1,0:T(8,128)(2,1)} %a_hbm.1, ...), custom_call_target="tpu_custom_call" | custom-call | flops 2147483648 | bytes 2097152 | tf_op jit(solution)/shard_map/pallas_call | solution.py:439
  37.0 1.1 %broadcast_multiply_fusion = f32[512,512]{1,0:T(8,128)} fusion(f32[512,512]{1,0:T(8,128)S(1)} %get-tuple-element.7, f32[512]{0:T(512)S(1)} %bitcast.1), kind=kLoop, calls=%fused_computation | loop fusion | flops 262144 | bytes 2099200 | tf_op jit(solution)/shard_map/mul | solution.py:474

commit v6 on v4

--- a/solution.py
+++ b/solution.py
@@ -16,7 +16,7 @@
 TILE = 128
 STEP = 2
 PARTS = KA // 2 // STEP
-WINDOW = 2
+WINDOW = 4
 LAG = 2
 MESH = pl.DeviceIdType.MESH
 
@@ -167,7 +167,7 @@
                     a_copy(p, t // PARTS, t % PARTS, True).start()
 
         for s in range(SECTIONS):
-            c = t - WINDOW * s
+            c = t - PARTS * s
             if 0 <= c < PARTS:
 
                 @pl.when(row == n_row - SECTIONS + s)

time: 38 us -> 39.9 us (1.050)
  Pallas kernels: 36.1 us -> 38 us
    pallas_call x1, Pallas kernels: 36.1 us -> 38 us  [local(): pl.pallas_call(functools.partial(kernel, n_row, n_col), out_shape=(pltpu....]
where the time goes in v6:
time: 39.9 us; the launch traced here: 39.8 us
  Pallas kernels  38 us (95%)
  other arithmetic  1.1 us (3%)
  between operations  0.66 us (2%)
    pallas_call x1, Pallas kernels, local(): pl.pallas_call(functools.partial(kernel, n_row, n_col), out_shape=(pltpu....  38 us
    mul x1, other arithmetic, local(): return kept * scale  1.1 us

profile of v6, /device:TPU:0, one launch (start us, length us, event | category | flops | bytes accessed | tf_op | source)
XLA Modules:
  0.0 39.8 jit_solution(6788454295982324902)
XLA Ops:
  0.7 38.0 %shard_map.82 = (f32[512,512]{1,0:T(8,128)S(1)}, f32[1,512]{1,0:T(1,128)S(1)}) custom-call(s32[1,1,2,16]{3,2,1,0:T(2,128)} %ai_hbm.1, s32[1,1,2]{2,1,0:T(1,128)} %ac_hbm.1, s32[1,1,16]{2,1,0:T(1,128)} %bi_hbm.1, s32[1,1]{1,0:T(1,128)S(6)} %copy.9.bc_hbm, s32[4,4]{1,0:T(4,128)} %mask_hbm.1, bf16[1,1,2,16,128,128]{5,4,3,2,1,0:T(8,128)(2,1)} %a_hbm.1, ...), custom_call_target="tpu_custom_call" | custom-call | flops 2147483648 | bytes 2097152 | tf_op jit(solution)/shard_map/pallas_call | solution.py:435
  38.7 1.1 %broadcast_multiply_fusion = f32[512,512]{1,0:T(8,128)} fusion(f32[512,512]{1,0:T(8,128)S(1)} %get-tuple-element.7, f32[512]{0:T(512)S(1)} %bitcast.1), kind=kLoop, calls=%fused_computation | loop fusion | flops 262144 | bytes 2099200 | tf_op jit(solution)/shard_map/mul | solution.py:470

commit v7 on v4

--- a/solution.py
+++ b/solution.py
@@ -18,6 +18,7 @@
 PARTS = KA // 2 // STEP
 WINDOW = 2
 LAG = 2
+AHEAD = 2
 MESH = pl.DeviceIdType.MESH
 
 
@@ -301,7 +302,7 @@
             b_root_sibling(s).wait_recv()
 
     most = LAG * max(n_col - 3, last_pair - 1, 0)
-    for t in range(PARTS + most):
+    for t in range(PARTS + most + AHEAD):
         forward(t)
 
     @pl.when(positions[0] == n_col - 1)
@@ -351,8 +352,8 @@
         section_ready(s)
         make_table(s)
         for j in range(PARTS):
-            if s + 1 < SECTIONS:
-                forward(PARTS + most + j)
+            if s + 1 < SECTIONS and j < PARTS - AHEAD:
+                forward(PARTS + most + AHEAD + j)
             product(s, j)
 
     partial = jnp.zeros((1, NB * TILE), jnp.float32)

time: 38 us -> 38.3 us (level)
  no operation moved by 1% of the time
where the time goes in v7:
time: 38.3 us; the launch traced here: 38.1 us
  Pallas kernels  36.4 us (95%)
  other arithmetic  1.1 us (3%)
  between operations  0.66 us (2%)
    pallas_call x1, Pallas kernels, local(): pl.pallas_call(functools.partial(kernel, n_row, n_col), out_shape=(pltpu....  36.4 us
    mul x1, other arithmetic, local(): return kept * scale  1.1 us

profile of v7, /device:TPU:0, one launch (start us, length us, event | category | flops | bytes accessed | tf_op | source)
XLA Modules:
  0.0 38.1 jit_solution(6375763365533677525)
XLA Ops:
  0.7 36.4 %shard_map.82 = (f32[512,512]{1,0:T(8,128)S(1)}, f32[1,512]{1,0:T(1,128)S(1)}) custom-call(s32[1,1,2,16]{3,2,1,0:T(2,128)} %ai_hbm.1, s32[1,1,2]{2,1,0:T(1,128)} %ac_hbm.1, s32[1,1,16]{2,1,0:T(1,128)} %bi_hbm.1, s32[1,1]{1,0:T(1,128)S(6)} %copy.9.bc_hbm, s32[4,4]{1,0:T(4,128)} %mask_hbm.1, bf16[1,1,2,16,128,128]{5,4,3,2,1,0:T(8,128)(2,1)} %a_hbm.1, ...), custom_call_target="tpu_custom_call" | custom-call | flops 2147483648 | bytes 2097152 | tf_op jit(solution)/shard_map/pallas_call | solution.py:436
  37.0 1.1 %broadcast_multiply_fusion = f32[512,512]{1,0:T(8,128)} fusion(f32[512,512]{1,0:T(8,128)S(1)} %get-tuple-element.7, f32[512]{0:T(512)S(1)} %bitcast.1), kind=kLoop, calls=%fused_computation | loop fusion | flops 262144 | bytes 2099200 | tf_op jit(solution)/shard_map/mul | solution.py:471
